TPU v7x, 32 devices: a whole 2x2x4 slice. The times are simulated.
32 devices in a mesh: dp: 8 (over z, x), head: 4 (over y, core).
Axes of the slice: x: 2, y: 2, z: 4, core: 2. Of those that a mesh axis runs over, the one named last changes fastest.
Arguments:
- key_grads: bfloat16 [2, 4096, 2048], P(None, 'dp', 'head'), may hold values from -6 to 6
- value_grads: bfloat16 [2, 4096, 2048], P(None, 'dp', 'head'), may hold values from -6 to 6
- key_weight: bfloat16 [2, 3584, 2048], P(None, 'dp', 'head'), may hold values from -0.125 to 0.125
- value_weight: bfloat16 [2, 3584, 2048], P(None, 'dp', 'head'), may hold values from -0.125 to 0.125
- block_source: int32 [64], replicated, may hold values from 0 to 63, as said below
- hidden_mid: bfloat16 [4096, 3584], P('dp', 'head')
- mlp_out: bfloat16 [4096, 3584], P('dp', 'head')
- post_gain: bfloat16 [3584], P('head'), may hold values from 0.5 to 2
- final_gain: bfloat16 [3584], P('head'), may hold values from 0.5 to 2
- gate_pre: bfloat16 [4096, 7168], P('dp', 'head'), may hold values from -6 to 6
- up_pre: bfloat16 [4096, 7168], P('dp', 'head'), may hold values from -6 to 6
- down_weight: bfloat16 [7168, 3584], P('head', 'dp'), may hold values from -0.09375 to 0.09375
Outputs:
- resid_grad: bfloat16 [4096, 3584], P('dp', 'head')
- gate_grad: bfloat16 [4096, 7168], P('dp', 'head')
- up_grad: bfloat16 [4096, 7168], P('dp', 'head')
Inputs may be any that keep to these rules, and one draw needn't show every extreme that they name: block_source is a permutation of the 64 row blocks. The decoder blocks of one device are blocks 8 * a to 8 * a + 7, and the encoder blocks of device b are blocks 8 * b to 8 * b + 7; at most 2 decoder blocks of one device fill encoder blocks of one device, and exactly 2 do for some pairs of devices in every draw.
All inputs are finite; a program needn't handle non-finite values.
Results may differ from a plain program's by a relative error of at most 0.02.
Values may be sent and summed in bfloat16 or wider, within the bound.
A program may use at most 64 MiB of HBM per device.

v0:
```python
import jax
import jax.numpy as jnp
from jax import lax
from jax.sharding import PartitionSpec as P

CAP = 2


epsilon = 1e-06


def gelu_parts(gate_value):
    activated, pullback = jax.vjp(
        lambda pre_act: jax.nn.gelu(pre_act, approximate=True), gate_value
    )
    return (activated, pullback(jnp.ones_like(gate_value))[0])


def repack(dec_memory, block_source, dev_blocks):
    row_count, col_share = dec_memory.shape
    block_rows = row_count // dev_blocks
    total_blocks = dev_blocks * dev_blocks
    slot_count = dev_blocks * CAP
    this_dev = lax.axis_index("dp")
    block_ids = jnp.arange(total_blocks, dtype=jnp.int32)
    is_source = block_source[:, None] == block_ids[None, :]
    dest_block = jnp.sum(jnp.where(is_source, block_ids[:, None], 0), axis=0)
    dest_device = (dest_block // dev_blocks).reshape(dev_blocks, dev_blocks)
    same_dest = dest_device[:, :, None] == dest_device[:, None, :]
    slot_ids = jnp.arange(dev_blocks, dtype=jnp.int32)
    before_slot = slot_ids[None, :] < slot_ids[:, None]
    dest_rank = jnp.sum((same_dest & before_slot[None, :, :]).astype(jnp.int32), axis=2)
    own_dest = lax.dynamic_index_in_dim(dest_device, this_dev, 0, keepdims=False)
    own_rank = lax.dynamic_index_in_dim(dest_rank, this_dev, 0, keepdims=False)
    send_slot = own_dest * CAP + own_rank
    buffer_ids = jnp.arange(slot_count, dtype=jnp.int32)
    send_pick = (buffer_ids[:, None] == send_slot[None, :]).astype(jnp.bfloat16)
    local_rows = dec_memory.reshape(dev_blocks, block_rows * col_share)
    outgoing = jnp.dot(send_pick, local_rows, preferred_element_type=jnp.float32).astype(
        jnp.bfloat16
    )
    outgoing = outgoing.reshape(dev_blocks, CAP * block_rows, col_share)
    incoming = lax.all_to_all(outgoing, "dp", split_axis=0, concat_axis=0, tiled=True)
    own_sources = lax.dynamic_slice_in_dim(block_source, this_dev * dev_blocks, dev_blocks)
    source_device = own_sources // dev_blocks
    flat_ranks = dest_rank.reshape(-1)
    source_rank = jnp.sum(
        jnp.where(block_ids[None, :] == own_sources[:, None], flat_ranks[None, :], 0), axis=1
    )
    recv_slot = source_device * CAP + source_rank
    recv_pick = (recv_slot[:, None] == buffer_ids[None, :]).astype(jnp.bfloat16)
    arrived = incoming.reshape(slot_count, block_rows * col_share)
    placed = jnp.dot(recv_pick, arrived, preferred_element_type=jnp.float32).astype(jnp.bfloat16)
    return placed.reshape(row_count, col_share)


def per_device(
    key_grads,
    value_grads,
    key_weight,
    value_weight,
    block_source,
    hidden_mid,
    mlp_out,
    post_gain,
    final_gain,
    gate_pre,
    up_pre,
    down_weight,
):
    row_count, col_share = hidden_mid.shape
    width = col_share * lax.axis_size("head")
    dev_blocks = lax.axis_size("dp")
    key_piece = lax.all_gather(key_weight, "dp", axis=1, tiled=True)
    value_piece = lax.all_gather(value_weight, "dp", axis=1, tiled=True)
    term = jnp.einsum("lrk,lck->rc", key_grads, key_piece, preferred_element_type=jnp.float32)
    term = term + jnp.einsum(
        "lrk,lck->rc", value_grads, value_piece, preferred_element_type=jnp.float32
    )
    dec_memory = lax.psum_scatter(
        term.astype(jnp.bfloat16), "head", scatter_dimension=1, tiled=True
    )
    memory_grad = repack(dec_memory, block_source, dev_blocks)
    mid_value = hidden_mid.astype(jnp.float32)
    out_value = mlp_out.astype(jnp.float32)
    gain_post = post_gain.astype(jnp.float32)
    gain_final = final_gain.astype(jnp.float32)
    sum_out = lax.psum(jnp.sum(out_value * out_value, axis=1), "head")
    out_scale = lax.rsqrt(sum_out / width + epsilon)[:, None]
    resid = mid_value + out_value * out_scale * gain_post
    sum_resid = lax.psum(jnp.sum(resid * resid, axis=1), "head")
    resid_scale = lax.rsqrt(sum_resid / width + epsilon)[:, None]
    norm_grad = memory_grad.astype(jnp.float32) * gain_final
    final_dot = lax.psum(jnp.sum(norm_grad * resid, axis=1), "head")
    final_mean = resid_scale * final_dot[:, None] / width
    resid_total = resid_scale * (norm_grad - resid * resid_scale * final_mean)
    post_input = resid_total * gain_post
    post_dot = lax.psum(jnp.sum(post_input * out_value, axis=1), "head")
    post_mean = out_scale * post_dot[:, None] / width
    post_grad = out_scale * (post_input - out_value * out_scale * post_mean)
    post_full = lax.all_gather(post_grad.astype(jnp.bfloat16), "head", axis=1, tiled=True)
    hidden_grad = lax.dot_general(
        post_full,
        lax.all_gather(down_weight, "dp", axis=1, tiled=True),
        (((1,), (1,)), ((), ())),
        preferred_element_type=jnp.float32,
    )
    activated, slope = gelu_parts(gate_pre.astype(jnp.float32))
    gate_grad = (hidden_grad * up_pre.astype(jnp.float32) * slope).astype(jnp.bfloat16)
    up_grad = (hidden_grad * activated).astype(jnp.bfloat16)
    return (resid_total.astype(jnp.bfloat16), gate_grad, up_grad)


def solution(mesh):
    return jax.shard_map(
        per_device,
        mesh=mesh,
        in_specs=(
            P(None, "dp", "head"),
            P(None, "dp", "head"),
            P(None, "dp", "head"),
            P(None, "dp", "head"),
            P(),
            P("dp", "head"),
            P("dp", "head"),
            P("head"),
            P("head"),
            P("dp", "head"),
            P("dp", "head"),
            P("head", "dp"),
        ),
        out_specs=(P("dp", "head"), P("dp", "head"), P("dp", "head")),
        check_vma=False,
    )
```

profile of v0, /device:TPU:28, one launch (start us, length us, event | category | flops | bytes accessed | tf_op | source)
XLA Modules:
  0.0 563.5 jit_solution(847038242452561185)
XLA Ops:
  7.2 0.0 copy-start
  7.2 0.0 all-gather.5.cloned.1.call-start
  7.2 0.7 all-gather.5.cloned.1.call-update
  7.9 0.0 all-gather.7.cloned.1.call-start
  8.0 0.7 all-gather.7.cloned.1.call-update
  8.7 0.0 copy-start.7
  8.7 0.0 reduce-scatter.4.cloned.1.call-start
  8.7 112.5 %all-gather.5.cloned.1.call-done = bf16[2,3584,512]{2,1,0:T(8,128)(2,1)} async-done(((bf16[2,448,512]{2,1,0:T(8,128)(2,1)}), bf16[2,3584,512]{2,1,0:T(8,128)(2,1)}) %all-gather.5.cloned.1.call-update) | async-done | bytes 7340048 | tf_op jit(solution)/shard_map/all_gather | solution.py:74
  121.2 0.0 copy-done
  121.2 9.2 %fusion.25 = f32[512,3584,1]{1,0,2:T(8,128)} fusion(bf16[2,512,512]{2,1,0:T(8,128)(2,1)S(1)} %copy-done, bf16[2,3584,512]{2,1,0:T(8,128)(2,1)} %all-gather.5.cloned.1.call-done), kind=kOutput, calls=%fused_computation.62 | convolution fusion | flops 3758096384 | bytes 15728640 | tf_op jit(solution)/shard_map/lrk,lck->rc/dot_general | solution.py:76
  130.4 103.2 %all-gather.7.cloned.1.call-done = bf16[2,3584,512]{2,1,0:T(8,128)(2,1)} async-done(((bf16[2,448,512]{2,1,0:T(8,128)(2,1)}), bf16[2,3584,512]{2,1,0:T(8,128)(2,1)}) %all-gather.7.cloned.1.call-update) | async-done | bytes 7340048 | tf_op jit(solution)/shard_map/all_gather | solution.py:75
  233.6 9.7 %fusion.1 = bf16[512,3584]{1,0:T(8,128)(2,1)} fusion(f32[512,3584,1]{1,0,2:T(8,128)} %fusion.25, bf16[2,512,512]{2,1,0:T(8,128)(2,1)S(1)} %copy-done.7, bf16[2,3584,512]{2,1,0:T(8,128)(2,1)} %all-gather.7.cloned.1.call-done), kind=kOutput, calls=%fused_computation.4 | convolution fusion | flops 3761766400 | bytes 19398656 | tf_op jit(solution)/shard_map/lrk,lck->rc/dot_general | solution.py:77
  243.3 5.9 %copy.15 = bf16[512,3584]{0,1:T(8,128)(2,1)} copy(bf16[512,3584]{1,0:T(8,128)(2,1)} %fusion.1) | data formatting | bytes 7340032
  249.2 0.0 reduce-scatter.4.cloned.1.call-update
  249.3 0.0 all-gather.11.cloned.1.call-start
  249.3 0.5 all-gather.11.cloned.1.call-update
  249.9 0.0 copy-done.5
  249.9 0.1 select_reduce_fusion
  250.0 0.1 reduce_sum.68
  250.1 0.3 convert_reduce_fusion
  250.4 39.5 %reduce-scatter.4.cloned.1.call-done = bf16[896,512]{1,0:T(8,128)(2,1)} async-done(((bf16[3584,512]{1,0:T(8,128)(2,1)}), bf16[896,512]{1,0:T(8,128)(2,1)}) %reduce-scatter.4.cloned.1.call-update) | async-done | bytes 917520
  289.9 1.5 copy.16
  291.4 1.3 reshape.102
  292.8 1.8 convolution_convert_fusion
  294.6 1.8 reshape.103
  296.4 6.1 %all-to-all-start = ((bf16[8,128,896]{2,1,0:T(8,128)(2,1)}), bf16[8,128,896]{2,1,0:T(8,128)(2,1)S(1)}, u32[]{:S(2)}, u32[]{:S(2)}) async-start(bf16[8,128,896]{2,1,0:T(8,128)(2,1)} %reshape.103), calls=%async_computation | async-start | bytes 3670016 | tf_op jit(solution)/shard_map/all_to_all | solution.py:43
  302.5 0.0 all-gather.9.cloned.1.call-start
  302.5 0.1 broadcast_in_dim.28
  302.6 0.1 dynamic_slice.10
  302.7 0.0 copy-done.4
  302.7 0.3 fusion.19
  302.9 6.4 %psum.28 = f32[512]{0:T(512)S(1)} all-reduce(f32[512]{0:T(512)S(1)} %fusion.19), channel_id=1, replica_groups=mesh['dp'=8,'head'=4] {'head'}, use_global_device_ids=true, to_apply=%region_1.2 | all-reduce | flops 512 | bytes 4096 | tf_op jit(solution)/shard_map/psum | solution.py:88
  309.3 0.2 select_reduce_fusion.1
  309.5 0.1 multiply_add_fusion
  309.6 78.3 %all-to-all-done = bf16[8,128,896]{2,1,0:T(8,128)(2,1)S(1)} async-done(((bf16[8,128,896]{2,1,0:T(8,128)(2,1)}), bf16[8,128,896]{2,1,0:T(8,128)(2,1)S(1)}, u32[]{:S(2)}, u32[]{:S(2)}) %all-to-all-start) | async-done | bytes 1835040 | tf_op jit(solution)/shard_map/all_to_all | solution.py:43
  387.9 1.8 reshape.104
  389.7 3.2 fusion
  392.8 1.8 reshape.105
  394.6 2.0 multiply_reduce_fusion.1
  396.6 6.8 %all-reduce = (f32[512]{0:T(512)S(1)}, f32[512]{0:T(512)S(1)}) all-reduce(f32[512]{0:T(512)S(1)} %get-tuple-element.4, f32[512]{0:T(512)S(1)} %get-tuple-element.3), channel_id=1, replica_groups=mesh['dp'=8,'head'=4] {'head'}, use_global_device_ids=true, to_apply=%region_9.10 | all-reduce | flops 1024 | bytes 8192 | tf_op jit(solution)/shard_map/psum | solution.py:94
  403.5 3.6 fusion.20
  407.1 6.2 %psum.31 = f32[512]{0:T(512)S(1)} all-reduce(f32[512]{0:T(512)S(1)} %get-tuple-element.7), channel_id=1, replica_groups=mesh['dp'=8,'head'=4] {'head'}, use_global_device_ids=true, to_apply=%region_11.12 | all-reduce | flops 512 | bytes 4096 | tf_op jit(solution)/shard_map/psum | solution.py:98
  413.3 3.9 fusion.18
  417.2 0.0 all-gather.9.cloned.1.call-update
  417.2 91.3 %all-gather.11.cloned.1.call-done = bf16[1792,3584]{0,1:T(8,128)(2,1)} async-done(((bf16[1792,448]{0,1:T(8,128)(2,1)}), bf16[1792,3584]{0,1:T(8,128)(2,1)}) %all-gather.11.cloned.1.call-update) | async-done | bytes 12845072 | tf_op jit(solution)/shard_map/all_gather | solution.py:104
  508.5 32.8 %all-gather.9.cloned.1.call-done = bf16[512,3584]{1,0:T(8,128)(2,1)} async-done(((bf16[512,896]{1,0:T(8,128)(2,1)}), bf16[512,3584]{1,0:T(8,128)(2,1)}) %all-gather.9.cloned.1.call-update) | async-done | bytes 3670032 | tf_op jit(solution)/shard_map/all_gather | solution.py:101
  541.3 15.6 %fusion.12 = (bf16[512,1792]{1,0:T(8,128)(2,1)}, bf16[512,1792]{1,0:T(8,128)(2,1)}) fusion(bf16[512,1792]{1,0:T(8,128)(2,1)S(1)} %copy-done.6, bf16[512,1792]{1,0:T(8,128)(2,1)} %param.22, bf16[512,3584]{1,0:T(8,128)(2,1)} %all-gather.9.cloned.1.call-done, bf16[1792,3584]{0,1:T(8,128)(2,1)} %all-gather.11.cloned.1.call-done), kind=kOutput, calls=%fused_computation.20 | convolution fusion | flops 6599606272 | bytes 23855104 | tf_op jit(solution)/shard_map/dot_general | solution.py:102
  556.9 0.0 copy-done.1
  (18 shorter events, 0.1 us)
Async XLA Ops:
  7.2 114.1 %copy-start = (bf16[2,512,512]{2,1,0:T(8,128)(2,1)S(1)}, bf16[2,512,512]{2,1,0:T(8,128)(2,1)}, u32[]{:S(2)}) copy-start(bf16[2,512,512]{2,1,0:T(8,128)(2,1)} %param.12) | copy-start | bytes 3145732
  7.2 114.1 %all-gather.5.cloned.1.call-start = ((), (), s32[]{:S(2)}) async-start(), calls=%async_computation.2 | async-start | bytes 8257536 | tf_op jit(solution)/shard_map/all_gather | solution.py:74
  7.9 225.7 %all-gather.7.cloned.1.call-start = ((), (), s32[]{:S(2)}) async-start(), calls=%async_computation.3 | async-start | bytes 8257536 | tf_op jit(solution)/shard_map/all_gather | solution.py:75
  8.7 225.0 %copy-start.7 = (bf16[2,512,512]{2,1,0:T(8,128)(2,1)S(1)}, bf16[2,512,512]{2,1,0:T(8,128)(2,1)}, u32[]{:S(2)}) copy-start(bf16[2,512,512]{2,1,0:T(8,128)(2,1)} %param.13) | copy-start | bytes 3145732
  8.7 281.2 %reduce-scatter.4.cloned.1.call-start = ((), (), s32[]{:S(2)}) async-start(), calls=%async_computation.6 | async-start | bytes 4587520
  249.2 0.7 copy-start.5
  249.3 259.3 %all-gather.11.cloned.1.call-start = ((), (), s32[]{:S(2)}) async-start(), calls=%async_computation.5 | async-start | bytes 14450688 | tf_op jit(solution)/shard_map/all_gather | solution.py:104
  296.3 6.3 %copy-start.3 = (bf16[896]{0:T(1024)(128)(2,1)S(1)}, bf16[896]{0:T(1024)(128)(2,1)}, u32[]{:S(2)}) copy-start(bf16[896]{0:T(1024)(128)(2,1)} %param.19) | copy-start | bytes 5380
  296.4 6.3 %copy-start.4 = (bf16[896]{0:T(1024)(128)(2,1)S(1)}, bf16[896]{0:T(1024)(128)(2,1)}, u32[]{:S(2)}) copy-start(bf16[896]{0:T(1024)(128)(2,1)} %param.20) | copy-start | bytes 5380
  296.4 6.3 %copy-start.2 = (bf16[512,896]{1,0:T(8,128)(2,1)S(1)}, bf16[512,896]{1,0:T(8,128)(2,1)}, u32[]{:S(2)}) copy-start(bf16[512,896]{1,0:T(8,128)(2,1)} %param.18) | copy-start | bytes 2752516
  296.4 91.5 %all-to-all-start = ((bf16[8,128,896]{2,1,0:T(8,128)(2,1)}), bf16[8,128,896]{2,1,0:T(8,128)(2,1)S(1)}, u32[]{:S(2)}, u32[]{:S(2)}) async-start(bf16[8,128,896]{2,1,0:T(8,128)(2,1)} %reshape.103), calls=%async_computation | async-start | bytes 3670016 | tf_op jit(solution)/shard_map/all_to_all | solution.py:43
  302.5 238.8 %all-gather.9.cloned.1.call-start = ((), (), s32[]{:S(2)}) async-start(), calls=%async_computation.4 | async-start | bytes 4587520 | tf_op jit(solution)/shard_map/all_gather | solution.py:101
  413.3 128.0 %copy-start.6 = (bf16[512,1792]{1,0:T(8,128)(2,1)S(1)}, bf16[512,1792]{1,0:T(8,128)(2,1)}, u32[]{:S(2)}) copy-start(bf16[512,1792]{1,0:T(8,128)(2,1)} %param.21) | copy-start | bytes 5505028
  541.3 15.6 %copy-start.1 = (bf16[2,512,512]{2,1,0:T(8,128)(2,1)S(1)}, bf16[2,512,512]{2,1,0:T(8,128)(2,1)}, u32[]{:S(2)}) copy-start(bf16[2,512,512]{2,1,0:T(8,128)(2,1)} %param.12) | copy-start | bytes 3145732
Sparse Core Ops, SparseCore 0:
  10.2 110.9 all-gather.4
  123.4 110.1 all-gather.6
  249.4 40.4 reduce-scatter.3
  292.2 216.3 all-gather.10
  510.6 30.6 all-gather.8
where the time goes:
time: 567 us; the launch traced here: 563 us
  waiting for transfers between devices  460 us (81%)
  matrix products  39.4 us (7%)
  blocking collectives  19.4 us (3%)
  local copies, waits for them, and re-layouts  14.5 us (3%)
  between operations  13.9 us (2%)
  other arithmetic  10.4 us (2%)
  starting transfers between devices  6.3 us (1%)
    all_gather x1, waiting for transfers between devices, per_device(): key_piece = lax.all_gather(key_weight, 'dp', axis=1, tiled=True)  113 us
    all_gather x1, waiting for transfers between devices, per_device(): value_piece = lax.all_gather(value_weight, 'dp', axis=1, tiled=True)  103 us
    all_gather x1, waiting for transfers between devices, per_device(): lax.all_gather(down_weight, 'dp', axis=1, tiled=True)  91.3 us
    all_to_all x1, waiting for transfers between devices, repack(): lax.all_to_all(outgoing, 'dp', split_axis=0, concat_axis=0, tiled=True)  78.3 us
    unnamed x6, waiting for transfers between devices  41.4 us
    all_gather x1, waiting for transfers between devices, per_device(): lax.all_gather(post_grad.astype(jnp.bfloat16), 'head', axis=1, tiled=True)  32.8 us
    dot_general x1, matrix products, per_device(): lax.dot_general(post_full, lax.all_gather(down_weight, 'dp', axis=1, tile...  15.6 us
  transfers between devices with their start and end apart: 6, of which 6 were waited for; matrix products, arithmetic and copies ran while one was open for 6% of the time, Pallas kernels for 0%

commit v1 on v0

--- a/solution.py
+++ b/solution.py
@@ -1,6 +1,10 @@
+import functools
+
 import jax
 import jax.numpy as jnp
 from jax import lax
+from jax.experimental import pallas as pl
+from jax.experimental.pallas import tpu as pltpu
 from jax.sharding import PartitionSpec as P
 
 CAP = 2
@@ -111,9 +115,551 @@
     return (resid_total.astype(jnp.bfloat16), gate_grad, up_grad)
 
 
+MESH = pl.DeviceIdType.MESH
+N_DEV = 32
+TILE = 64
+
+
+def remote(src, dst, send_sem, recv_sem, dp_index, head_index):
+    return pltpu.make_async_remote_copy(
+        src_ref=src,
+        dst_ref=dst,
+        send_sem=send_sem,
+        recv_sem=recv_sem,
+        device_id=(dp_index, head_index),
+        device_id_type=MESH,
+    )
+
+
+def memory_kernel(
+    key_grads,
+    value_grads,
+    key_weight,
+    value_weight,
+    send_index,
+    recv_index,
+    mid_ref,
+    out_ref,
+    post_ref,
+    final_ref,
+    resid_grad,
+    post_full,
+    a_buf,
+    b_buf,
+    part,
+    core_send,
+    core_recv,
+    y_send,
+    y_recv,
+    dec,
+    slots_out,
+    slots_in,
+    mem,
+    resid,
+    cols,
+    rows_buf,
+    stat,
+    red_out,
+    red_in,
+    a_loc,
+    a_ss,
+    a_rs,
+    b_loc,
+    b_ss,
+    b_rs,
+    x_ss,
+    x_rs,
+    c_ss,
+    c_rs,
+    y_ss,
+    y_rs,
+    s_loc,
+    s_ss,
+    s_rs,
+    r_ss,
+    r_rs,
+    p_ss,
+    p_rs,
+    q_ss,
+    q_rs,
+):
+    row_count, col_share = mid_ref.shape
+    width = col_share * 4
+    w_rows = key_weight.shape[1]
+    dp = lax.axis_index("dp")
+    hd = lax.axis_index("head")
+    z, x = dp // 2, dp % 2
+    y, core = hd // 2, hd % 2
+    n_group, z_par = z % 2, z % 2
+    me = dp * 4 + hd
+
+    barrier = pltpu.get_barrier_semaphore()
+
+    @pl.loop(0, N_DEV)
+    def _(i):
+        @pl.when(i != me)
+        def _():
+            pl.semaphore_signal(barrier, inc=1, device_id=(i // 4, i % 4), device_id_type=MESH)
+
+    pl.semaphore_wait(barrier, N_DEV - 1)
+
+    grads = (key_grads.at[0], key_grads.at[1], value_grads.at[0], value_grads.at[1])
+    weights = (key_weight.at[0], key_weight.at[1], value_weight.at[0], value_weight.at[1])
+    own_half = pl.ds(pl.multiple_of(x * w_rows, 64), w_rows)
+    other_half = pl.ds(pl.multiple_of((1 - x) * w_rows, 64), w_rows)
+
+    def b_send(k, t):
+        target = z // 2 + 2 * t
+        return target, remote(
+            weights[k],
+            b_buf.at[z_par, k, own_half],
+            b_ss.at[t, k],
+            b_rs.at[z_par, k],
+            target * 2 + x,
+            hd,
+        )
+
+    def a_send(k):
+        return remote(
+            grads[k], a_buf.at[z_par, k], a_ss.at[k], a_rs.at[k], (z + 1 - 2 * z_par) * 2 + x, hd
+        )
+
+    def a_local(k):
+        return pltpu.make_async_copy(grads[k], a_buf.at[z_par, k], a_loc.at[k])
+
+    def b_local(j, k):
+        return pltpu.make_async_copy(weights[k], b_buf.at[j, k, own_half], b_loc.at[k])
+
+    def x_send(j, k):
+        block = b_buf.at[j, k, own_half]
+        return remote(block, block, x_ss.at[j, k], x_rs.at[j, k], dp + 1 - 2 * x, hd)
+
+    def for_source(j, k, start):
+        is_own = 2 * n_group + j == z
+
+        @pl.when(is_own)
+        def _():
+            if start:
+                b_local(j, k).start()
+            else:
+                b_local(j, k).wait()
+
+        if not start:
+
+            @pl.when(jnp.logical_not(is_own))
+            def _():
+                block = b_buf.at[j, k, own_half]
+                pltpu.make_async_copy(block, block, b_rs.at[j, k]).wait()
+
+    for k in range(4):
+        for t in range(2):
+            target, copy = b_send(k, t)
+            pl.when(target != z)(copy.start)
+        for j in range(2):
+            for_source(j, k, True)
+        a_send(k).start()
+        a_local(k).start()
+
+    def forward(k):
+        for j in range(2):
+            for_source(j, k, False)
+            x_send(j, k).start()
+
+    forward(0)
+
+    def exchange(turn):
+        rows_t = jnp.transpose(cols[...])
+        red_out[turn] = rows_t[0:8]
+        copies = []
+        for i in range(3):
+            copies.append(
+                remote(
+                    red_out.at[turn],
+                    red_in.at[turn, i],
+                    r_ss.at[turn, i],
+                    r_rs.at[turn, i],
+                    dp,
+                    lax.rem(hd + 1 + i, 4),
+                )
+            )
+        for copy in copies:
+            copy.start()
+        for copy in copies:
+            copy.wait()
+        rows_buf[...] = jnp.zeros_like(rows_buf)
+        rows_buf[0:8] = red_out[turn] + red_in[turn, 0] + red_in[turn, 1] + red_in[turn, 2]
+        stat[turn] = jnp.transpose(rows_buf[...])
+
+    def lanes(first, second):
+        lane = lax.broadcasted_iota(jnp.int32, (TILE, 128), 1)
+        return jnp.where(lane == 0, first, jnp.where(lane == 1, second, 0.0))
+
+    def tile(i):
+        return pl.ds(pl.multiple_of(i * TILE, TILE), TILE)
+
+    def row_sum(values):
+        return jnp.sum(values, axis=1, keepdims=True)
+
+    def out_scale_of(rows):
+        return lax.rsqrt(stat[0, rows, 0:1] / width + epsilon)
+
+    def resid_scale_of(rows):
+        return lax.rsqrt(stat[1, rows, 0:1] / width + epsilon)
+
+    @pl.loop(0, row_count // TILE)
+    def _(i):
+        rows = tile(i)
+        out_value = out_ref[rows].astype(jnp.float32)
+        total = row_sum(out_value * out_value)
+        cols[rows] = lanes(total, total)
+
+    exchange(0)
+    gain_post = post_ref[...].astype(jnp.float32)
+    gain_final = final_ref[...].astype(jnp.float32)
+
+    forward(1)
+
+    @pl.loop(0, row_count // TILE)
+    def _(i):
+        rows = tile(i)
+        scaled = out_ref[rows].astype(jnp.float32) * gain_post
+        value = mid_ref[rows].astype(jnp.float32) + scaled * out_scale_of(rows)
+        resid[rows] = value
+        cols[rows] = lanes(row_sum(value * value), row_sum(value * scaled))
+
+    exchange(1)
+
+    forward(2)
+    forward(3)
+
+    for k in range(4):
+        a_local(k).wait()
+        a_send(k).wait_recv()
+        for j in range(2):
+            block = b_buf.at[j, k, other_half]
+            pltpu.make_async_copy(block, block, x_rs.at[j, k]).wait()
+
+    def product(r, j, rows):
+        total = None
+        for k in range(4):
+            term = lax.dot_general(
+                a_buf[r, k, rows, :],
+                b_buf[j, k],
+                (((1,), (1,)), ((), ())),
+                preferred_element_type=jnp.float32,
+            )
+            total = term if total is None else total + term
+        return total
+
+    def core_copy(r):
+        return remote(
+            core_send.at[r], core_recv.at[r], c_ss.at[r], c_rs.at[r], dp, hd + 1 - 2 * core
+        )
+
+    MM = 256
+    for step in range(2):
+        r = (1 - y) if step == 0 else y
+
+        @pl.loop(0, row_count // MM)
+        def _(i):
+            rows = pl.ds(pl.multiple_of(i * MM, MM), MM)
+            core_send[r, rows, :] = product(r, 1 - core, rows).astype(jnp.bfloat16)
+
+        core_copy(r).start()
+
+    def y_copy(part_id):
+        rows = pl.ds(part_id * MM, MM)
+        return remote(
+            y_send.at[rows],
+            y_recv.at[rows],
+            y_ss.at[part_id],
+            y_rs.at[part_id],
+            dp,
+            hd + 2 - 4 * y,
+        )
+
+    @pl.loop(0, row_count // MM)
+    def _(i):
+        rows = pl.ds(pl.multiple_of(i * MM, MM), MM)
+        part[rows, :] = product(1 - y, core, rows)
+
+    core_copy(1 - y).wait()
+    for piece in range(2):
+        rows = pl.ds(piece * MM, MM)
+        y_send[rows, :] = (
+            part[rows, :] + core_recv[1 - y, rows, :].astype(jnp.float32)
+        ).astype(jnp.bfloat16)
+        y_copy(piece).start()
+
+    @pl.loop(0, row_count // MM)
+    def _(i):
+        rows = pl.ds(pl.multiple_of(i * MM, MM), MM)
+        part[rows, :] = product(y, core, rows)
+
+    core_copy(y).wait()
+    for piece in range(2):
+        y_copy(piece).wait()
+
+    @pl.loop(0, row_count // TILE)
+    def _(i):
+        rows = tile(i)
+        total = part[rows, :] + core_recv[y, rows, :].astype(jnp.float32)
+        dec[i] = (total + y_recv[rows, :].astype(jnp.float32)).astype(jnp.bfloat16)
+
+    chunk = 2 * (2 * (z // 2) + y) + x
+    to_head = 2 * n_group + core
+
+    def slot_copy(i):
+        return remote(
+            slots_out.at[pl.ds(2 * i, 2)],
+            slots_in.at[pl.ds(2 * chunk, 2)],
+            s_ss.at[i],
+            s_rs.at[chunk],
+            i,
+            to_head,
+        )
+
+    def slot_local(i):
+        return pltpu.make_async_copy(
+            slots_out.at[pl.ds(2 * i, 2)], slots_in.at[pl.ds(2 * chunk, 2)], s_loc
+        )
+
+    def is_me(i):
+        return jnp.logical_and(i == dp, to_head == hd)
+
+    @pl.loop(0, 8)
+    def _(step):
+        i = lax.rem(dp + 1 + step, 8)
+        for s in range(2):
+            slots_out[2 * i + s] = dec[send_index[(chunk * 8 + i) * 2 + s]]
+
+        @pl.when(is_me(i))
+        def _():
+            slot_local(i).start()
+
+        @pl.when(jnp.logical_not(is_me(i)))
+        def _():
+            slot_copy(i).start()
+
+    @pl.loop(0, 8)
+    def _(rho):
+        src_z = 2 * (rho // 4) + hd // 2
+        src_dp = 2 * src_z + rho % 2
+        src_head = 2 * ((rho // 2) % 2) + hd % 2
+        own = jnp.logical_and(src_dp == dp, src_head == hd)
+        block = slots_in.at[pl.ds(2 * rho, 2)]
+
+        @pl.when(own)
+        def _():
+            slot_local(dp).wait()
+
+        @pl.when(jnp.logical_not(own))
+        def _():
+            pltpu.make_async_copy(block, block, s_rs.at[rho]).wait()
+
+    @pl.loop(0, row_count // TILE)
+    def _(i):
+        rows = tile(i)
+        block = slots_in[recv_index[dp * 8 + i]]
+        mem[i] = block
+        norm_grad = block.astype(jnp.float32) * gain_final
+        scaled = out_ref[rows].astype(jnp.float32) * gain_post
+        cols[rows] = lanes(row_sum(norm_grad * resid[rows]), row_sum(norm_grad * scaled))
+
+    exchange(2)
+
+    own_cols = pl.ds(pl.multiple_of(hd * col_share, 128), col_share)
+    y_head = hd + 2 - 4 * y
+    core_head = hd + 1 - 2 * core
+    y_cols = pl.ds(pl.multiple_of(y_head * col_share, 128), col_share)
+    core_cols = pl.ds(pl.multiple_of(core_head * col_share, 128), col_share)
+    far_cols = pl.ds(pl.multiple_of((3 - hd) * col_share, 128), col_share)
+    PIECE = 128
+
+    def across_y(piece):
+        block = post_full.at[pl.ds(piece * PIECE, PIECE), own_cols]
+        return remote(block, block, p_ss.at[0, piece], p_rs.at[0, piece], dp, y_head)
+
+    def across_core(piece):
+        block = post_full.at[pl.ds(piece * PIECE, PIECE), own_cols]
+        return remote(block, block, p_ss.at[1, piece], p_rs.at[1, piece], dp, core_head)
+
+    def pass_on(piece):
+        block = post_full.at[pl.ds(piece * PIECE, PIECE), y_cols]
+        return remote(block, block, q_ss.at[piece], q_rs.at[piece], dp, core_head)
+
+    for piece in range(row_count // PIECE):
+
+        @pl.loop(piece * (PIECE // TILE), (piece + 1) * (PIECE // TILE))
+        def _(i):
+            rows = tile(i)
+            out_scale = out_scale_of(rows)
+            resid_scale = resid_scale_of(rows)
+            final_mean = resid_scale * stat[2, rows, 0:1] / width
+            post_dot = resid_scale * (
+                stat[2, rows, 1:2] - resid_scale * final_mean * stat[1, rows, 1:2]
+            )
+            post_mean = out_scale * post_dot / width
+            out_value = out_ref[rows].astype(jnp.float32)
+            norm_grad = mem[i].astype(jnp.float32) * gain_final
+            total = resid_scale * (norm_grad - resid[rows] * (resid_scale * final_mean))
+            resid_grad[rows, :] = total.astype(jnp.bfloat16)
+            post_grad = out_scale * (total * gain_post - out_value * (out_scale * post_mean))
+            post_full[rows, own_cols] = post_grad.astype(jnp.bfloat16)
+
+        across_y(piece).start()
+        across_core(piece).start()
+
+    for piece in range(row_count // PIECE):
+        block = post_full.at[pl.ds(piece * PIECE, PIECE), y_cols]
+        pltpu.make_async_copy(block, block, p_rs.at[0, piece]).wait()
+        pass_on(piece).start()
+
+    for piece in range(row_count // PIECE):
+        near = post_full.at[pl.ds(piece * PIECE, PIECE), core_cols]
+        pltpu.make_async_copy(near, near, p_rs.at[1, piece]).wait()
+        far = post_full.at[pl.ds(piece * PIECE, PIECE), far_cols]
+        pltpu.make_async_copy(far, far, q_rs.at[piece]).wait()
+        across_y(piece).wait_send()
+        across_core(piece).wait_send()
+        pass_on(piece).wait_send()
+
+    for k in range(4):
+        for t in range(2):
+            target, copy = b_send(k, t)
+            pl.when(target != z)(copy.wait_send)
+        a_send(k).wait_send()
+        for j in range(2):
+            x_send(j, k).wait_send()
+
+    @pl.loop(0, 8)
+    def _(i):
+        @pl.when(jnp.logical_not(is_me(i)))
+        def _():
+            slot_copy(i).wait_send()
+
+
+def block_tables(block_source):
+    blocks = jnp.arange(64, dtype=jnp.int32)
+    is_source = block_source[:, None] == blocks[None, :]
+    dest_block = jnp.sum(jnp.where(is_source, blocks[:, None], 0), axis=0)
+    dest = (dest_block // 8).reshape(8, 8)
+    ids = jnp.arange(8, dtype=jnp.int32)
+    same = dest[:, :, None] == dest[:, None, :]
+    rank = jnp.sum((same & (ids[None, :] < ids[:, None])[None]).astype(jnp.int32), axis=2)
+    slot = dest * CAP + rank
+    slot_ids = jnp.arange(16, dtype=jnp.int32)
+    taken = slot[:, :, None] == slot_ids[None, None, :]
+    send_index = jnp.sum(jnp.where(taken, ids[None, :, None], 0), axis=1).reshape(128)
+    source_rank = jnp.sum(jnp.where(is_source, rank.reshape(1, 64), 0), axis=1)
+    recv_index = (block_source // 8) * CAP + source_rank
+    return send_index, recv_index
+
+
+def fused_device(
+    key_grads,
+    value_grads,
+    key_weight,
+    value_weight,
+    block_source,
+    hidden_mid,
+    mlp_out,
+    post_gain,
+    final_gain,
+    gate_pre,
+    up_pre,
+    down_weight,
+):
+    row_count, col_share = hidden_mid.shape
+    depth = key_grads.shape[2]
+    send_index, recv_index = block_tables(block_source)
+    half = jnp.bfloat16
+    single = jnp.float32
+    dma = pltpu.SemaphoreType.DMA
+    anywhere = pl.BlockSpec(memory_space=pl.ANY)
+    vmem = pl.BlockSpec(memory_space=pltpu.VMEM)
+    smem = pl.BlockSpec(memory_space=pltpu.SMEM)
+    resid_grad, post_full = pl.pallas_call(
+        memory_kernel,
+        out_shape=(
+            jax.ShapeDtypeStruct((row_count, col_share), half),
+            jax.ShapeDtypeStruct((row_count, col_share * 4), half),
+        ),
+        in_specs=[anywhere] * 4 + [smem] * 2 + [vmem] * 4,
+        out_specs=(vmem, vmem),
+        scratch_shapes=[
+            pltpu.VMEM((2, 4, row_count, depth), half),
+            pltpu.VMEM((2, 4, col_share, depth), half),
+            pltpu.VMEM((row_count, col_share), single),
+            pltpu.VMEM((2, row_count, col_share), half),
+            pltpu.VMEM((2, row_count, col_share), half),
+            pltpu.VMEM((row_count, col_share), half),
+            pltpu.VMEM((row_count, col_share), half),
+            pltpu.VMEM((8, TILE, col_share), half),
+            pltpu.VMEM((16, TILE, col_share), half),
+            pltpu.VMEM((16, TILE, col_share), half),
+            pltpu.VMEM((8, TILE, col_share), half),
+            pltpu.VMEM((row_count, col_share), single),
+            pltpu.VMEM((row_count, 128), single),
+            pltpu.VMEM((128, row_count), single),
+            pltpu.VMEM((3, row_count, 128), single),
+            pltpu.VMEM((3, 8, row_count), single),
+            pltpu.VMEM((3, 3, 8, row_count), single),
+            dma((4,)),
+            dma((4,)),
+            dma((4,)),
+            dma((4,)),
+            dma((2, 4)),
+            dma((2, 4)),
+            dma((2, 4)),
+            dma((2, 4)),
+            dma((2,)),
+            dma((2,)),
+            dma((2,)),
+            dma((2,)),
+            dma,
+            dma((8,)),
+            dma((8,)),
+            dma((3, 3)),
+            dma((3, 3)),
+            dma((2, 4)),
+            dma((2, 4)),
+            dma((4,)),
+            dma((4,)),
+        ],
+        cost_estimate=pl.CostEstimate(
+            flops=100_000_000_000, bytes_accessed=400_000_000, transcendentals=0
+        ),
+        compiler_params=pltpu.CompilerParams(
+            collective_id=0, has_side_effects=True, vmem_limit_bytes=52 * 1024 * 1024
+        ),
+    )(
+        key_grads,
+        value_grads,
+        key_weight,
+        value_weight,
+        send_index,
+        recv_index,
+        hidden_mid,
+        mlp_out,
+        post_gain[None, :],
+        final_gain[None, :],
+    )
+    hidden_grad = lax.dot_general(
+        post_full,
+        lax.all_gather(down_weight, "dp", axis=1, tiled=True),
+        (((1,), (1,)), ((), ())),
+        preferred_element_type=jnp.float32,
+    )
+    activated, slope = gelu_parts(gate_pre.astype(jnp.float32))
+    gate_grad = (hidden_grad * up_pre.astype(jnp.float32) * slope).astype(jnp.bfloat16)
+    up_grad = (hidden_grad * activated).astype(jnp.bfloat16)
+    return (resid_grad, gate_grad, up_grad)
+
+
 def solution(mesh):
     return jax.shard_map(
-        per_device,
+        fused_device if mesh.shape["dp"] == 8 and mesh.shape["head"] == 4 else per_device,
         mesh=mesh,
         in_specs=(
             P(None, "dp", "head"),

time: 567 us -> 359 us (0.63)
  waiting for transfers between devices: 460 us -> 0.7 us
  Pallas kernels: 0 us -> 317 us
  matrix products: 39.4 us -> 15.6 us
  blocking collectives: 19.4 us -> 0 us
  local copies, waits for them, and re-layouts: 14.5 us -> 3.72 us
  other arithmetic: 10.4 us -> 2.65 us
  starting transfers between devices: 6.3 us -> 0.04 us
    all_gather x4 -> x1, waiting for transfers between devices: 340 us -> 0.02 us  [fused_device(): lax.all_gather(down_weight, 'dp', axis=1, tiled=True)]
    pallas_call x0 -> x1, Pallas kernels: none -> 317 us  [fused_device(): pl.pallas_call(memory_kernel, out_shape=(jax.ShapeDtypeStruct((row_count,...]
    all_to_all x1 -> x0, waiting for transfers between devices: 78.3 us -> none  [repack(): lax.all_to_all(outgoing, 'dp', split_axis=0, concat_axis=0, tiled=True)]
    unnamed x6 -> x1, waiting for transfers between devices: 41.4 us -> 0.68 us
    dot_general x5 -> x1, matrix products: 39.4 us -> 15.6 us  [fused_device(): lax.dot_general(post_full, lax.all_gather(down_weight, 'dp', axis=1, tile...]
    psum x3 -> x0, blocking collectives: 19.4 us -> none  [the longest x1 6.84 us: per_device(): final_dot = lax.psum(jnp.sum(norm_grad * resid, axis=1), 'head')]
    all_to_all x1 -> x0, starting transfers between devices: 6.14 us -> none  [repack(): lax.all_to_all(outgoing, 'dp', split_axis=0, concat_axis=0, tiled=True)]
  transfers between devices with their start and end apart: 6 -> 1, of which waited for: 6 -> 0; matrix products, arithmetic and copies ran while one was open for 6% -> 1% of each run, Pallas kernels for 0% -> 90%
where the time goes in v1:
time: 359 us; the launch traced here: 354 us
  Pallas kernels  317 us (88%)
  matrix products  15.6 us (4%)
  between operations  14.1 us (4%)
  local copies, waits for them, and re-layouts  3.72 us (1%)
    pallas_call x1, Pallas kernels, fused_device(): pl.pallas_call(memory_kernel, out_shape=(jax.ShapeDtypeStruct((row_count,...  317 us
    dot_general x1, matrix products, fused_device(): lax.dot_general(post_full, lax.all_gather(down_weight, 'dp', axis=1, tile...  15.6 us
  transfers between devices with their start and end apart: 1, of which 0 were waited for; matrix products, arithmetic and copies ran while one was open for 1% of the time, Pallas kernels for 90%

profile of v1, /device:TPU:28, one launch (start us, length us, event | category | flops | bytes accessed | tf_op | source)
XLA Modules:
  0.0 354.0 jit_solution(3111687735073771735)
XLA Ops:
  7.2 0.0 all-gather.2.cloned.1.call-start
  7.2 0.7 all-gather.2.cloned.1.call-update
  7.9 0.7 select_reduce_fusion.2
  8.6 0.1 reduce_sum.39
  8.7 0.3 convert_reduce_fusion
  9.0 0.1 broadcast_in_dim.55
  9.1 0.1 select_reduce_fusion.1
  9.2 0.1 reshape.95.send_index
  9.3 0.7 broadcast_in_dim.57.post_ref
  10.0 0.7 broadcast_in_dim.58.final_ref
  10.7 0.8 select_reduce_fusion
  11.5 0.7 multiply_add_fusion.1.recv_index
  12.2 0.0 copy-start
  12.2 1.2 copy-done
  13.4 0.0 copy-start.1
  13.4 317.2 %shard_map.139 = (bf16[512,896]{1,0:T(8,128)(2,1)S(1)}, bf16[512,3584]{1,0:T(8,128)(2,1)}) custom-call(bf16[2,512,512]{2,1,0:T(8,128)(2,1)} %key_grads.1, bf16[2,512,512]{2,1,0:T(8,128)(2,1)} %value_grads.1, bf16[2,448,512]{2,1,0:T(8,128)(2,1)S(1)} %copy-done, bf16[2,448,512]{2,1,0:T(8,128)(2,1)} %value_weight.1, s32[128]{0:T(128)S(1)} %reshape.95.send_index, ...), custom_call_target="tpu_custom_call" | custom-call | flops 99999997952 | bytes 400000000 | tf_op jit(solution)/shard_map/pallas_call | solution.py:582
  330.6 0.0 all-gather.2.cloned.1.call-done
  330.6 0.0 copy-done.1
  330.6 15.6 %fusion.10 = (bf16[512,1792]{1,0:T(8,128)(2,1)}, bf16[512,1792]{1,0:T(8,128)(2,1)}) fusion(bf16[512,1792]{1,0:T(8,128)(2,1)S(1)} %copy-done.1, bf16[512,1792]{1,0:T(8,128)(2,1)} %param.22, bf16[512,3584]{1,0:T(8,128)(2,1)} %get-tuple-element.6, bf16[1792,3584]{0,1:T(8,128)(2,1)} %all-gather.2.cloned.1.call-done), kind=kOutput, calls=%fused_computation.15 | convolution fusion | flops 6599606272 | bytes 23855104 | tf_op jit(solution)/shard_map/dot_general | solution.py:648
  346.2 0.9 copy.16
  (3 shorter events, 0.0 us)
Async XLA Ops:
  7.2 323.5 %all-gather.2.cloned.1.call-start = ((), (), s32[]{:S(2)}) async-start(), calls=%async_computation | async-start | bytes 14450688 | tf_op jit(solution)/shard_map/all_gather | solution.py:650
  12.2 1.2 copy-start
  13.4 317.3 %copy-start.1 = (bf16[512,1792]{1,0:T(8,128)(2,1)S(1)}, bf16[512,1792]{1,0:T(8,128)(2,1)}, u32[]{:S(2)}) copy-start(bf16[512,1792]{1,0:T(8,128)(2,1)} %param.21) | copy-start | bytes 5505028
Sparse Core Ops, SparseCore 0:
  10.2 294.6 all-gather.1

commit v2 on v1

--- a/solution.py
+++ b/solution.py
@@ -118,6 +118,10 @@
 MESH = pl.DeviceIdType.MESH
 N_DEV = 32
 TILE = 64
+HID = 256
+EARLY = 3
+ROOT = 0.7978845608028654
+CUBIC = 0.044715
 
 
 def remote(src, dst, send_sem, recv_sem, dp_index, head_index):
@@ -142,8 +146,12 @@
     out_ref,
     post_ref,
     final_ref,
+    down_ref,
+    gate_ref,
+    up_ref,
     resid_grad,
-    post_full,
+    gate_grad,
+    up_grad,
     a_buf,
     b_buf,
     part,
@@ -182,6 +190,18 @@
     p_rs,
     q_ss,
     q_rs,
+    post_buf,
+    down_buf,
+    acc,
+    pre_in,
+    grad_out,
+    dl_s,
+    dz_ss,
+    dz_rs,
+    dx_ss,
+    dx_rs,
+    pre_s,
+    grad_s,
 ):
     row_count, col_share = mid_ref.shape
     width = col_share * 4
@@ -264,6 +284,66 @@
         for j in range(2):
             for_source(j, k, False)
             x_send(j, k).start()
+
+    def hidden(p):
+        return pl.ds(p * HID, HID)
+
+    def down_local(p):
+        return pltpu.make_async_copy(
+            down_ref.at[hidden(p)], down_buf.at[dp, hidden(p)], dl_s.at[p]
+        )
+
+    def down_send(t, p):
+        return remote(
+            down_ref.at[hidden(p)],
+            down_buf.at[dp, hidden(p)],
+            dz_ss.at[t - 1, p],
+            dz_rs.at[z, p],
+            lax.rem(z + t, 4) * 2 + x,
+            hd,
+        )
+
+    def down_across(src_z, p):
+        block = down_buf.at[2 * src_z + x, hidden(p)]
+        return remote(block, block, dx_ss.at[src_z, p], dx_rs.at[src_z, p], dp + 1 - 2 * x, hd)
+
+    def down_start(p):
+        for t in (1, 3, 2):
+            down_send(t, p).start()
+        down_local(p).wait()
+        down_across(z, p).start()
+
+    def down_forward(p):
+        for t in (1, 3, 2):
+            src_z = lax.rem(z + t, 4)
+            block = down_buf.at[2 * src_z + x, hidden(p)]
+            pltpu.make_async_copy(block, block, dz_rs.at[src_z, p]).wait()
+            down_across(src_z, p).start()
+
+    def pre_copies(p):
+        cols_p = hidden(p)
+        return (
+            pltpu.make_async_copy(gate_ref.at[:, cols_p], pre_in.at[0, p % 2], pre_s.at[0, p % 2]),
+            pltpu.make_async_copy(up_ref.at[:, cols_p], pre_in.at[1, p % 2], pre_s.at[1, p % 2]),
+        )
+
+    def grad_copies(p):
+        cols_p = hidden(p)
+        return (
+            pltpu.make_async_copy(
+                grad_out.at[0, p % 2], gate_grad.at[:, cols_p], grad_s.at[0, p % 2]
+            ),
+            pltpu.make_async_copy(
+                grad_out.at[1, p % 2], up_grad.at[:, cols_p], grad_s.at[1, p % 2]
+            ),
+        )
+
+    n_hid = down_ref.shape[0] // HID
+    for p in range(n_hid):
+        down_local(p).start()
+    for p in range(2):
+        for copy in pre_copies(p):
+            copy.start()
 
     forward(0)
 
@@ -339,6 +419,9 @@
             block = b_buf.at[j, k, other_half]
             pltpu.make_async_copy(block, block, x_rs.at[j, k]).wait()
 
+    for p in range(EARLY):
+        down_start(p)
+
     def product(r, j, rows):
         total = None
         for k in range(4):
@@ -406,6 +489,7 @@
         total = part[rows, :] + core_recv[y, rows, :].astype(jnp.float32)
         dec[i] = (total + y_recv[rows, :].astype(jnp.float32)).astype(jnp.bfloat16)
 
+    down_forward(0)
     chunk = 2 * (2 * (z // 2) + y) + x
     to_head = 2 * n_group + core
 
@@ -441,6 +525,10 @@
         def _():
             slot_copy(i).start()
 
+    for p in range(EARLY, n_hid):
+        down_start(p)
+    down_forward(1)
+
     @pl.loop(0, 8)
     def _(rho):
         src_z = 2 * (rho // 4) + hd // 2
@@ -456,6 +544,8 @@
         @pl.when(jnp.logical_not(own))
         def _():
             pltpu.make_async_copy(block, block, s_rs.at[rho]).wait()
+
+    down_forward(2)
 
     @pl.loop(0, row_count // TILE)
     def _(i):
@@ -468,24 +558,20 @@
 
     exchange(2)
 
-    own_cols = pl.ds(pl.multiple_of(hd * col_share, 128), col_share)
     y_head = hd + 2 - 4 * y
     core_head = hd + 1 - 2 * core
-    y_cols = pl.ds(pl.multiple_of(y_head * col_share, 128), col_share)
-    core_cols = pl.ds(pl.multiple_of(core_head * col_share, 128), col_share)
-    far_cols = pl.ds(pl.multiple_of((3 - hd) * col_share, 128), col_share)
     PIECE = 128
 
     def across_y(piece):
-        block = post_full.at[pl.ds(piece * PIECE, PIECE), own_cols]
+        block = post_buf.at[pl.ds(2 * hd, 2), pl.ds(piece * PIECE, PIECE)]
         return remote(block, block, p_ss.at[0, piece], p_rs.at[0, piece], dp, y_head)
 
     def across_core(piece):
-        block = post_full.at[pl.ds(piece * PIECE, PIECE), own_cols]
+        block = post_buf.at[pl.ds(2 * hd, 2), pl.ds(piece * PIECE, PIECE)]
         return remote(block, block, p_ss.at[1, piece], p_rs.at[1, piece], dp, core_head)
 
     def pass_on(piece):
-        block = post_full.at[pl.ds(piece * PIECE, PIECE), y_cols]
+        block = post_buf.at[pl.ds(2 * y_head, 2), pl.ds(piece * PIECE, PIECE)]
         return remote(block, block, q_ss.at[piece], q_rs.at[piece], dp, core_head)
 
     for piece in range(row_count // PIECE):
@@ -505,24 +591,81 @@
             total = resid_scale * (norm_grad - resid[rows] * (resid_scale * final_mean))
             resid_grad[rows, :] = total.astype(jnp.bfloat16)
             post_grad = out_scale * (total * gain_post - out_value * (out_scale * post_mean))
-            post_full[rows, own_cols] = post_grad.astype(jnp.bfloat16)
+            post_half = post_grad.astype(jnp.bfloat16)
+            post_buf[2 * hd, rows, :] = post_half[:, : col_share // 2]
+            post_buf[2 * hd + 1, rows, :] = post_half[:, col_share // 2 :]
 
         across_y(piece).start()
         across_core(piece).start()
 
     for piece in range(row_count // PIECE):
-        block = post_full.at[pl.ds(piece * PIECE, PIECE), y_cols]
+        block = post_buf.at[pl.ds(2 * y_head, 2), pl.ds(piece * PIECE, PIECE)]
         pltpu.make_async_copy(block, block, p_rs.at[0, piece]).wait()
         pass_on(piece).start()
+        down_forward(3 + piece)
 
     for piece in range(row_count // PIECE):
-        near = post_full.at[pl.ds(piece * PIECE, PIECE), core_cols]
+        near = post_buf.at[pl.ds(2 * core_head, 2), pl.ds(piece * PIECE, PIECE)]
         pltpu.make_async_copy(near, near, p_rs.at[1, piece]).wait()
-        far = post_full.at[pl.ds(piece * PIECE, PIECE), far_cols]
+        far = post_buf.at[pl.ds(2 * (3 - hd), 2), pl.ds(piece * PIECE, PIECE)]
         pltpu.make_async_copy(far, far, q_rs.at[piece]).wait()
+
+    for p in range(n_hid):
+        for src_z in range(4):
+            block = down_buf.at[2 * src_z + 1 - x, hidden(p)]
+            pltpu.make_async_copy(block, block, dx_rs.at[src_z, p]).wait()
+
+        total = None
+        for c in range(8):
+            term = lax.dot_general(
+                post_buf[c],
+                down_buf[c, hidden(p), :],
+                (((1,), (1,)), ((), ())),
+                preferred_element_type=jnp.float32,
+            )
+            total = term if total is None else total + term
+        acc[...] = total
+        for copy in pre_copies(p):
+            copy.wait()
+        if p >= 2:
+            for copy in grad_copies(p - 2):
+                copy.wait()
+
+        @pl.loop(0, row_count // TILE)
+        def _(i):
+            rows = tile(i)
+            grad = acc[rows, :]
+            value = pre_in[0, p % 2, rows, :].astype(jnp.float32)
+            other = pre_in[1, p % 2, rows, :].astype(jnp.float32)
+            square = value * value
+            bent = jnp.tanh(ROOT * value * (1.0 + CUBIC * square))
+            share = 0.5 * (1.0 + bent)
+            slope = share + 0.5 * value * (1.0 - bent * bent) * (
+                ROOT * (1.0 + 3.0 * CUBIC * square)
+            )
+            grad_out[0, p % 2, rows, :] = (grad * other * slope).astype(jnp.bfloat16)
+            grad_out[1, p % 2, rows, :] = (grad * (value * share)).astype(jnp.bfloat16)
+
+        for copy in grad_copies(p):
+            copy.start()
+        if p + 2 < n_hid:
+            for copy in pre_copies(p + 2):
+                copy.start()
+
+    for p in range(n_hid - 2, n_hid):
+        for copy in grad_copies(p):
+            copy.wait()
+
+    for piece in range(row_count // PIECE):
         across_y(piece).wait_send()
         across_core(piece).wait_send()
         pass_on(piece).wait_send()
+
+    for p in range(n_hid):
+        for t in (1, 2, 3):
+            down_send(t, p).wait_send()
+        for src_z in range(4):
+            down_across(src_z, p).wait_send()
 
     for k in range(4):
         for t in range(2):
@@ -579,14 +722,16 @@
     anywhere = pl.BlockSpec(memory_space=pl.ANY)
     vmem = pl.BlockSpec(memory_space=pltpu.VMEM)
     smem = pl.BlockSpec(memory_space=pltpu.SMEM)
-    resid_grad, post_full = pl.pallas_call(
+    n_hid = down_weight.shape[0] // HID
+    return pl.pallas_call(
         memory_kernel,
         out_shape=(
             jax.ShapeDtypeStruct((row_count, col_share), half),
-            jax.ShapeDtypeStruct((row_count, col_share * 4), half),
+            jax.ShapeDtypeStruct(gate_pre.shape, half),
+            jax.ShapeDtypeStruct(gate_pre.shape, half),
         ),
-        in_specs=[anywhere] * 4 + [smem] * 2 + [vmem] * 4,
-        out_specs=(vmem, vmem),
+        in_specs=[anywhere] * 4 + [smem] * 2 + [vmem] * 4 + [anywhere] * 3,
+        out_specs=(vmem, anywhere, anywhere),
         scratch_shapes=[
             pltpu.VMEM((2, 4, row_count, depth), half),
             pltpu.VMEM((2, 4, col_share, depth), half),
@@ -626,12 +771,24 @@
             dma((2, 4)),
             dma((4,)),
             dma((4,)),
+            pltpu.VMEM((8, row_count, col_share // 2), half),
+            pltpu.VMEM((8,) + down_weight.shape, half),
+            pltpu.VMEM((row_count, HID), single),
+            pltpu.VMEM((2, 2, row_count, HID), half),
+            pltpu.VMEM((2, 2, row_count, HID), half),
+            dma((n_hid,)),
+            dma((3, n_hid)),
+            dma((4, n_hid)),
+            dma((4, n_hid)),
+            dma((4, n_hid)),
+            dma((2, 2)),
+            dma((2, 2)),
         ],
         cost_estimate=pl.CostEstimate(
             flops=100_000_000_000, bytes_accessed=400_000_000, transcendentals=0
         ),
         compiler_params=pltpu.CompilerParams(
-            collective_id=0, has_side_effects=True, vmem_limit_bytes=52 * 1024 * 1024
+            collective_id=0, has_side_effects=True, vmem_limit_bytes=60 * 1024 * 1024
         ),
     )(
         key_grads,
@@ -644,17 +801,10 @@
         mlp_out,
         post_gain[None, :],
         final_gain[None, :],
+        down_weight,
+        gate_pre,
+        up_pre,
     )
-    hidden_grad = lax.dot_general(
-        post_full,
-        lax.all_gather(down_weight, "dp", axis=1, tiled=True),
-        (((1,), (1,)), ((), ())),
-        preferred_element_type=jnp.float32,
-    )
-    activated, slope = gelu_parts(gate_pre.astype(jnp.float32))
-    gate_grad = (hidden_grad * up_pre.astype(jnp.float32) * slope).astype(jnp.bfloat16)
-    up_grad = (hidden_grad * activated).astype(jnp.bfloat16)
-    return (resid_grad, gate_grad, up_grad)
 
 
 def solution(mesh):

time: 359 us -> 369 us (1.028)
  Pallas kernels: 317 us -> 351 us
  matrix products: 15.6 us -> 0 us
  between operations: 14.1 us -> 0.67 us
  local copies, waits for them, and re-layouts: 3.72 us -> 12.7 us
    pallas_call x1, Pallas kernels: 317 us -> 351 us  [fused_device(): pl.pallas_call(memory_kernel, out_shape=(jax.ShapeDtypeStruct((row_count,...]
    dot_general x1 -> x0, matrix products: 15.6 us -> none  [fused_device(): lax.dot_general(post_full, lax.all_gather(down_weight, 'dp', axis=1, tile...]
    unnamed x5 -> x8, local copies, waits for them, and re-layouts: 2.1 us -> 9.42 us
  transfers between devices with their start and end apart: 1 -> 0, of which waited for: 0 -> 0; matrix products, arithmetic and copies ran while one was open for 1% -> 0% of each run, Pallas kernels for 90% -> 0%
where the time goes in v2:
time: 369 us; the launch traced here: 367 us
  Pallas kernels  351 us (95%)
  local copies, waits for them, and re-layouts  12.7 us (3%)
    pallas_call x1, Pallas kernels, fused_device(): pl.pallas_call(memory_kernel, out_shape=(jax.ShapeDtypeStruct((row_count,...  351 us
    unnamed x8, local copies, waits for them, and re-layouts  9.42 us

profile of v2, /device:TPU:28, one launch (start us, length us, event | category | flops | bytes accessed | tf_op | source)
XLA Modules:
  0.0 367.4 jit_solution(18285481774776580051)
XLA Ops:
  0.6 0.7 select_reduce_fusion.2
  1.4 0.1 reduce_sum.39
  1.5 1.3 broadcast_in_dim.57.post_ref
  2.7 1.3 broadcast_in_dim.58.final_ref
  4.0 0.3 convert_reduce_fusion
  4.3 0.1 broadcast_in_dim.55
  4.4 0.8 select_reduce_fusion
  5.2 1.2 multiply_add_fusion.1.recv_index
  6.5 0.1 select_reduce_fusion.1
  6.6 0.6 reshape.95.send_index
  7.2 3.7 %copy.16.down_ref = bf16[1792,448]{1,0:T(8,128)(2,1)} copy(bf16[1792,448]{0,1:T(8,128)(2,1)} %param.23) | data formatting | bytes 3211264 | tf_op args[11]
  10.9 350.9 %shard_map.139 = (bf16[512,896]{1,0:T(8,128)(2,1)}, bf16[512,1792]{1,0:T(8,128)(2,1)}, bf16[512,1792]{1,0:T(8,128)(2,1)}) custom-call(bf16[2,512,512]{2,1,0:T(8,128)(2,1)} %key_grads.1, bf16[2,512,512]{2,1,0:T(8,128)(2,1)} %value_grads.1, bf16[2,448,512]{2,1,0:T(8,128)(2,1)} %key_weight.1, bf16[2,448,512]{2,1,0:T(8,128)(2,1)} %value_weight.1, ...), custom_call_target="tpu_custom_call" | custom-call | flops 99999997952 | bytes 400000000 | tf_op jit(solution)/shard_map/pallas_call | solution.py:726
  361.7 0.0 copy-start.1
  361.7 2.3 copy.20
  364.1 0.0 copy-done.1
  364.1 0.0 copy-start
  364.1 1.2 copy.21
  365.3 0.9 copy-done
  366.2 1.2 copy.22
  (3 shorter events, 0.0 us)
Async XLA Ops:
  361.7 2.3 copy-start.1
  364.1 2.2 copy-start

commit v3 on v2

--- a/solution.py
+++ b/solution.py
@@ -277,6 +277,7 @@
             pl.when(target != z)(copy.start)
         for j in range(2):
             for_source(j, k, True)
+    for k in range(4):
         a_send(k).start()
         a_local(k).start()
 
@@ -290,13 +291,13 @@
 
     def down_local(p):
         return pltpu.make_async_copy(
-            down_ref.at[hidden(p)], down_buf.at[dp, hidden(p)], dl_s.at[p]
+            down_ref.at[:, hidden(p)], down_buf.at[dp, :, hidden(p)], dl_s.at[p]
         )
 
     def down_send(t, p):
         return remote(
-            down_ref.at[hidden(p)],
-            down_buf.at[dp, hidden(p)],
+            down_ref.at[:, hidden(p)],
+            down_buf.at[dp, :, hidden(p)],
             dz_ss.at[t - 1, p],
             dz_rs.at[z, p],
             lax.rem(z + t, 4) * 2 + x,
@@ -304,7 +305,7 @@
         )
 
     def down_across(src_z, p):
-        block = down_buf.at[2 * src_z + x, hidden(p)]
+        block = down_buf.at[2 * src_z + x, :, hidden(p)]
         return remote(block, block, dx_ss.at[src_z, p], dx_rs.at[src_z, p], dp + 1 - 2 * x, hd)
 
     def down_start(p):
@@ -316,7 +317,7 @@
     def down_forward(p):
         for t in (1, 3, 2):
             src_z = lax.rem(z + t, 4)
-            block = down_buf.at[2 * src_z + x, hidden(p)]
+            block = down_buf.at[2 * src_z + x, :, hidden(p)]
             pltpu.make_async_copy(block, block, dz_rs.at[src_z, p]).wait()
             down_across(src_z, p).start()
 
@@ -338,7 +339,7 @@
             ),
         )
 
-    n_hid = down_ref.shape[0] // HID
+    n_hid = down_ref.shape[1] // HID
     for p in range(n_hid):
         down_local(p).start()
     for p in range(2):
@@ -411,6 +412,8 @@
 
     forward(2)
     forward(3)
+    for p in range(EARLY):
+        down_start(p)
 
     for k in range(4):
         a_local(k).wait()
@@ -418,9 +421,6 @@
         for j in range(2):
             block = b_buf.at[j, k, other_half]
             pltpu.make_async_copy(block, block, x_rs.at[j, k]).wait()
-
-    for p in range(EARLY):
-        down_start(p)
 
     def product(r, j, rows):
         total = None
@@ -479,6 +479,7 @@
         rows = pl.ds(pl.multiple_of(i * MM, MM), MM)
         part[rows, :] = product(y, core, rows)
 
+    down_forward(0)
     core_copy(y).wait()
     for piece in range(2):
         y_copy(piece).wait()
@@ -489,7 +490,6 @@
         total = part[rows, :] + core_recv[y, rows, :].astype(jnp.float32)
         dec[i] = (total + y_recv[rows, :].astype(jnp.float32)).astype(jnp.bfloat16)
 
-    down_forward(0)
     chunk = 2 * (2 * (z // 2) + y) + x
     to_head = 2 * n_group + core
 
@@ -528,6 +528,7 @@
     for p in range(EARLY, n_hid):
         down_start(p)
     down_forward(1)
+    down_forward(2)
 
     @pl.loop(0, 8)
     def _(rho):
@@ -545,7 +546,7 @@
         def _():
             pltpu.make_async_copy(block, block, s_rs.at[rho]).wait()
 
-    down_forward(2)
+    down_forward(3)
 
     @pl.loop(0, row_count // TILE)
     def _(i):
@@ -598,11 +599,16 @@
         across_y(piece).start()
         across_core(piece).start()
 
+    down_forward(4)
+
     for piece in range(row_count // PIECE):
         block = post_buf.at[pl.ds(2 * y_head, 2), pl.ds(piece * PIECE, PIECE)]
         pltpu.make_async_copy(block, block, p_rs.at[0, piece]).wait()
         pass_on(piece).start()
-        down_forward(3 + piece)
+        if piece == 1:
+            down_forward(5)
+
+    down_forward(6)
 
     for piece in range(row_count // PIECE):
         near = post_buf.at[pl.ds(2 * core_head, 2), pl.ds(piece * PIECE, PIECE)]
@@ -612,15 +618,15 @@
 
     for p in range(n_hid):
         for src_z in range(4):
-            block = down_buf.at[2 * src_z + 1 - x, hidden(p)]
+            block = down_buf.at[2 * src_z + 1 - x, :, hidden(p)]
             pltpu.make_async_copy(block, block, dx_rs.at[src_z, p]).wait()
 
         total = None
         for c in range(8):
             term = lax.dot_general(
                 post_buf[c],
-                down_buf[c, hidden(p), :],
-                (((1,), (1,)), ((), ())),
+                down_buf[c, :, hidden(p)],
+                (((1,), (0,)), ((), ())),
                 preferred_element_type=jnp.float32,
             )
             total = term if total is None else total + term
@@ -683,19 +689,16 @@
 
 
 def block_tables(block_source):
-    blocks = jnp.arange(64, dtype=jnp.int32)
-    is_source = block_source[:, None] == blocks[None, :]
-    dest_block = jnp.sum(jnp.where(is_source, blocks[:, None], 0), axis=0)
-    dest = (dest_block // 8).reshape(8, 8)
-    ids = jnp.arange(8, dtype=jnp.int32)
-    same = dest[:, :, None] == dest[:, None, :]
-    rank = jnp.sum((same & (ids[None, :] < ids[:, None])[None]).astype(jnp.int32), axis=2)
-    slot = dest * CAP + rank
-    slot_ids = jnp.arange(16, dtype=jnp.int32)
-    taken = slot[:, :, None] == slot_ids[None, None, :]
-    send_index = jnp.sum(jnp.where(taken, ids[None, :, None], 0), axis=1).reshape(128)
-    source_rank = jnp.sum(jnp.where(is_source, rank.reshape(1, 64), 0), axis=1)
-    recv_index = (block_source // 8) * CAP + source_rank
+    places = jnp.arange(64, dtype=jnp.int32)
+    owner = block_source // 8
+    alike = (owner[:, None] == owner[None, :]) & ((places // 8)[:, None] == (places // 8)[None, :])
+    before = block_source[None, :] < block_source[:, None]
+    rank = jnp.sum((alike & before).astype(jnp.int32), axis=1)
+    recv_index = owner * CAP + rank
+    slot = (owner * 8 + places // 8) * CAP + rank
+    slots = jnp.arange(128, dtype=jnp.int32)
+    taken = slot[None, :] == slots[:, None]
+    send_index = jnp.sum(jnp.where(taken, (block_source % 8)[None, :], 0), axis=1)
     return send_index, recv_index
 
 
@@ -772,7 +775,7 @@
             dma((4,)),
             dma((4,)),
             pltpu.VMEM((8, row_count, col_share // 2), half),
-            pltpu.VMEM((8,) + down_weight.shape, half),
+            pltpu.VMEM((8,) + down_weight.shape[::-1], half),
             pltpu.VMEM((row_count, HID), single),
             pltpu.VMEM((2, 2, row_count, HID), half),
             pltpu.VMEM((2, 2, row_count, HID), half),
@@ -801,7 +804,7 @@
         mlp_out,
         post_gain[None, :],
         final_gain[None, :],
-        down_weight,
+        down_weight.T,
         gate_pre,
         up_pre,
     )

time: 369 us -> 323 us (0.88)
  Pallas kernels: 351 us -> 309 us
  local copies, waits for them, and re-layouts: 12.7 us -> 8.23 us
    pallas_call x1, Pallas kernels: 351 us -> 309 us  [fused_device(): pl.pallas_call(memory_kernel, out_shape=(jax.ShapeDtypeStruct((row_count,...]
    unnamed x8 -> x7, local copies, waits for them, and re-layouts: 9.42 us -> 5.7 us
where the time goes in v3:
time: 323 us; the launch traced here: 320 us
  Pallas kernels  309 us (96%)
  local copies, waits for them, and re-layouts  8.23 us (3%)
    pallas_call x1, Pallas kernels, fused_device(): pl.pallas_call(memory_kernel, out_shape=(jax.ShapeDtypeStruct((row_count,...  309 us

profile of v3, /device:TPU:28, one launch (start us, length us, event | category | flops | bytes accessed | tf_op | source)
XLA Modules:
  0.0 320.4 jit_solution(579187111488219116)
XLA Ops:
  0.6 0.7 and_select_fusion.2
  1.3 0.9 convert_reduce_fusion
  2.2 0.5 multiply_add_fusion
  2.7 0.6 select_reduce_fusion.send_index
  3.4 1.3 broadcast_in_dim.18.post_ref
  4.6 1.3 broadcast_in_dim.30.final_ref
  5.9 308.8 %shard_map.139 = (bf16[512,896]{1,0:T(8,128)(2,1)}, bf16[512,1792]{1,0:T(8,128)(2,1)}, bf16[512,1792]{1,0:T(8,128)(2,1)}) custom-call(bf16[2,512,512]{2,1,0:T(8,128)(2,1)} %key_grads.1, bf16[2,512,512]{2,1,0:T(8,128)(2,1)} %value_grads.1, bf16[2,448,512]{2,1,0:T(8,128)(2,1)} %key_weight.1, bf16[2,448,512]{2,1,0:T(8,128)(2,1)} %value_weight.1, ...), custom_call_target="tpu_custom_call" | custom-call | flops 99999997952 | bytes 400000000 | tf_op jit(solution)/shard_map/pallas_call | solution.py:729
  314.7 0.0 copy-start.1
  314.7 2.3 copy.18
  317.0 0.0 copy-done.1
  317.0 0.0 copy-start
  317.0 1.2 copy.19
  318.2 0.9 copy-done
  319.2 1.2 copy.20
Async XLA Ops:
  314.7 2.3 copy-start.1
  317.0 2.2 copy-start

commit v4 on v3

--- a/solution.py
+++ b/solution.py
@@ -120,6 +120,7 @@
 TILE = 64
 HID = 256
 EARLY = 3
+PLAIN = 4
 ROOT = 0.7978845608028654
 CUBIC = 0.044715
 
@@ -202,6 +203,13 @@
     dx_rs,
     pre_s,
     grad_s,
+    pair_buf,
+    pair_out,
+    pair_in,
+    pair_ss,
+    pair_rs,
+    half_ss,
+    half_rs,
 ):
     row_count, col_share = mid_ref.shape
     width = col_share * 4
@@ -312,14 +320,16 @@
         for t in (1, 3, 2):
             down_send(t, p).start()
         down_local(p).wait()
-        down_across(z, p).start()
+        if p < PLAIN:
+            down_across(z, p).start()
 
     def down_forward(p):
         for t in (1, 3, 2):
             src_z = lax.rem(z + t, 4)
             block = down_buf.at[2 * src_z + x, :, hidden(p)]
             pltpu.make_async_copy(block, block, dz_rs.at[src_z, p]).wait()
-            down_across(src_z, p).start()
+            if p < PLAIN:
+                down_across(src_z, p).start()
 
     def pre_copies(p):
         cols_p = hidden(p)
@@ -599,16 +609,33 @@
         across_y(piece).start()
         across_core(piece).start()
 
-    down_forward(4)
+    def half_send(i, block, dp_index, head_index):
+        return remote(block, block, half_ss.at[i], half_rs.at[i], dp_index, head_index)
+
+    x_half = remote(
+        post_buf.at[2 * hd + 1 - x],
+        pair_buf.at[hd],
+        half_ss.at[0],
+        half_rs.at[0],
+        dp + 1 - 2 * x,
+        hd,
+    )
+    x_half.start()
 
     for piece in range(row_count // PIECE):
         block = post_buf.at[pl.ds(2 * y_head, 2), pl.ds(piece * PIECE, PIECE)]
         pltpu.make_async_copy(block, block, p_rs.at[0, piece]).wait()
         pass_on(piece).start()
-        if piece == 1:
-            down_forward(5)
-
-    down_forward(6)
+
+    x_half.wait_recv()
+    y_half = half_send(1, pair_buf.at[hd], dp, y_head)
+    core_half = half_send(2, pair_buf.at[hd], dp, core_head)
+    y_half.start()
+    core_half.start()
+    near_half = pair_buf.at[y_head]
+    pltpu.make_async_copy(near_half, near_half, half_rs.at[1]).wait()
+    far_half = half_send(3, near_half, dp, core_head)
+    far_half.start()
 
     for piece in range(row_count // PIECE):
         near = post_buf.at[pl.ds(2 * core_head, 2), pl.ds(piece * PIECE, PIECE)]
@@ -616,20 +643,48 @@
         far = post_buf.at[pl.ds(2 * (3 - hd), 2), pl.ds(piece * PIECE, PIECE)]
         pltpu.make_async_copy(far, far, q_rs.at[piece]).wait()
 
-    for p in range(n_hid):
-        for src_z in range(4):
-            block = down_buf.at[2 * src_z + 1 - x, :, hidden(p)]
-            pltpu.make_async_copy(block, block, dx_rs.at[src_z, p]).wait()
-
+    def partial(left, first, count, step, p):
         total = None
-        for c in range(8):
+        for c in range(count):
             term = lax.dot_general(
-                post_buf[c],
-                down_buf[c, :, hidden(p)],
+                left(c),
+                down_buf[first + c * step, :, hidden(p)],
                 (((1,), (0,)), ((), ())),
                 preferred_element_type=jnp.float32,
             )
             total = term if total is None else total + term
+        return total
+
+    def pair_copy(p):
+        return remote(
+            pair_out.at[p - PLAIN],
+            pair_in.at[p - PLAIN],
+            pair_ss.at[p - PLAIN],
+            pair_rs.at[p - PLAIN],
+            dp + 1 - 2 * x,
+            hd,
+        )
+
+    for p in range(n_hid):
+        if p == PLAIN:
+            for i, owner in ((2, core_head), (3, 3 - hd)):
+                block = pair_buf.at[owner]
+                pltpu.make_async_copy(block, block, half_rs.at[i]).wait()
+            for later in range(PLAIN, n_hid):
+                down_forward(later)
+                pair_out[later - PLAIN] = partial(
+                    lambda c: pair_buf[c], x, 4, 2, later
+                ).astype(jnp.bfloat16)
+                pair_copy(later).start()
+        if p < PLAIN:
+            for src_z in range(4):
+                block = down_buf.at[2 * src_z + 1 - x, :, hidden(p)]
+                pltpu.make_async_copy(block, block, dx_rs.at[src_z, p]).wait()
+            total = partial(lambda c: post_buf[c], 0, 8, 1, p)
+        else:
+            total = partial(lambda c: post_buf[2 * c + x], x, 4, 2, p)
+            pair_copy(p).wait_recv()
+            total = total + pair_in[p - PLAIN].astype(jnp.float32)
         acc[...] = total
         for copy in pre_copies(p):
             copy.wait()
@@ -670,8 +725,13 @@
     for p in range(n_hid):
         for t in (1, 2, 3):
             down_send(t, p).wait_send()
-        for src_z in range(4):
-            down_across(src_z, p).wait_send()
+        if p < PLAIN:
+            for src_z in range(4):
+                down_across(src_z, p).wait_send()
+        else:
+            pair_copy(p).wait_send()
+    for copy in (x_half, y_half, core_half, far_half):
+        copy.wait_send()
 
     for k in range(4):
         for t in range(2):
@@ -786,6 +846,13 @@
             dma((4, n_hid)),
             dma((2, 2)),
             dma((2, 2)),
+            pltpu.VMEM((4, row_count, col_share // 2), half),
+            pltpu.VMEM((n_hid - PLAIN, row_count, HID), half),
+            pltpu.VMEM((n_hid - PLAIN, row_count, HID), half),
+            dma((n_hid - PLAIN,)),
+            dma((n_hid - PLAIN,)),
+            dma((4,)),
+            dma((4,)),
         ],
         cost_estimate=pl.CostEstimate(
             flops=100_000_000_000, bytes_accessed=400_000_000, transcendentals=0

time: 323 us -> 340 us (1.053)
  Pallas kernels: 309 us -> 323 us
    pallas_call x1, Pallas kernels: 309 us -> 323 us  [fused_device(): pl.pallas_call(memory_kernel, out_shape=(jax.ShapeDtypeStruct((row_count,...]
where the time goes in v4:
time: 340 us; the launch traced here: 335 us
  Pallas kernels  323 us (95%)
  local copies, waits for them, and re-layouts  8.23 us (2%)
    pallas_call x1, Pallas kernels, fused_device(): pl.pallas_call(memory_kernel, out_shape=(jax.ShapeDtypeStruct((row_count,...  323 us

profile of v4, /device:TPU:28, one launch (start us, length us, event | category | flops | bytes accessed | tf_op | source)
XLA Modules:
  0.0 335.1 jit_solution(11911630612357203796)
XLA Ops:
  0.6 0.7 and_select_fusion.2
  1.3 0.9 convert_reduce_fusion
  2.2 0.5 multiply_add_fusion
  2.7 0.6 select_reduce_fusion.send_index
  3.4 1.3 broadcast_in_dim.18.post_ref
  4.6 1.3 broadcast_in_dim.30.final_ref
  5.9 323.5 %shard_map.139 = (bf16[512,896]{1,0:T(8,128)(2,1)}, bf16[512,1792]{1,0:T(8,128)(2,1)}, bf16[512,1792]{1,0:T(8,128)(2,1)}) custom-call(bf16[2,512,512]{2,1,0:T(8,128)(2,1)} %key_grads.1, bf16[2,512,512]{2,1,0:T(8,128)(2,1)} %value_grads.1, bf16[2,448,512]{2,1,0:T(8,128)(2,1)} %key_weight.1, bf16[2,448,512]{2,1,0:T(8,128)(2,1)} %value_weight.1, ...), custom_call_target="tpu_custom_call" | custom-call | flops 99999997952 | bytes 400000000 | tf_op jit(solution)/shard_map/pallas_call | solution.py:789
  329.4 0.0 copy-start.1
  329.4 2.3 copy.18
  331.7 0.0 copy-done.1
  331.7 0.0 copy-start
  331.7 1.2 copy.19
  332.9 0.9 copy-done
  333.9 1.2 copy.20
Async XLA Ops:
  329.4 2.3 copy-start.1
  331.7 2.2 copy-start

commit v5 on v3

--- a/solution.py
+++ b/solution.py
@@ -546,8 +546,6 @@
         def _():
             pltpu.make_async_copy(block, block, s_rs.at[rho]).wait()
 
-    down_forward(3)
-
     @pl.loop(0, row_count // TILE)
     def _(i):
         rows = tile(i)
@@ -599,16 +597,15 @@
         across_y(piece).start()
         across_core(piece).start()
 
-    down_forward(4)
+    down_forward(3)
 
     for piece in range(row_count // PIECE):
         block = post_buf.at[pl.ds(2 * y_head, 2), pl.ds(piece * PIECE, PIECE)]
         pltpu.make_async_copy(block, block, p_rs.at[0, piece]).wait()
         pass_on(piece).start()
-        if piece == 1:
-            down_forward(5)
-
-    down_forward(6)
+
+    for p in range(EARLY + 1, n_hid):
+        down_forward(p)
 
     for piece in range(row_count // PIECE):
         near = post_buf.at[pl.ds(2 * core_head, 2), pl.ds(piece * PIECE, PIECE)]

time: 323 us -> 335 us (1.037)
  Pallas kernels: 309 us -> 323 us
    pallas_call x1, Pallas kernels: 309 us -> 323 us  [fused_device(): pl.pallas_call(memory_kernel, out_shape=(jax.ShapeDtypeStruct((row_count,...]
where the time goes in v5:
time: 335 us
  Pallas kernels  323 us (96%)
  local copies, waits for them, and re-layouts  8.23 us (2%)
    pallas_call x1, Pallas kernels, fused_device(): pl.pallas_call(memory_kernel, out_shape=(jax.ShapeDtypeStruct((row_count,...  323 us

profile of v5, /device:TPU:28, one launch (start us, length us, event | category | flops | bytes accessed | tf_op | source)
XLA Modules:
  0.0 335.0 jit_solution(18244319794214720016)
XLA Ops:
  0.6 0.7 and_select_fusion.2
  1.3 0.9 convert_reduce_fusion
  2.2 0.5 multiply_add_fusion
  2.7 0.6 select_reduce_fusion.send_index
  3.4 1.3 broadcast_in_dim.18.post_ref
  4.6 1.3 broadcast_in_dim.30.final_ref
  5.9 323.4 %shard_map.139 = (bf16[512,896]{1,0:T(8,128)(2,1)}, bf16[512,1792]{1,0:T(8,128)(2,1)}, bf16[512,1792]{1,0:T(8,128)(2,1)}) custom-call(bf16[2,512,512]{2,1,0:T(8,128)(2,1)} %key_grads.1, bf16[2,512,512]{2,1,0:T(8,128)(2,1)} %value_grads.1, bf16[2,448,512]{2,1,0:T(8,128)(2,1)} %key_weight.1, bf16[2,448,512]{2,1,0:T(8,128)(2,1)} %value_weight.1, ...), custom_call_target="tpu_custom_call" | custom-call | flops 99999997952 | bytes 400000000 | tf_op jit(solution)/shard_map/pallas_call | solution.py:726
  329.3 0.0 copy-start.1
  329.3 2.3 copy.18
  331.6 0.0 copy-done.1
  331.6 0.0 copy-start
  331.6 1.2 copy.19
  332.9 0.9 copy-done
  333.8 1.2 copy.20
Async XLA Ops:
  329.3 2.3 copy-start.1
  331.6 2.2 copy-start
